TPU v7x, 32 devices: a whole 2x2x4 slice. The times are simulated.
32 devices in a mesh: tok: 8 (over z, y), wid: 4 (over x, core).
Axes of the slice: x: 2, y: 2, z: 4, core: 2. Of those that a mesh axis runs over, the one named last changes fastest.
Arguments:
- queries: bfloat16 [1024, 8192], P('tok', 'wid'), may hold values from -6 to 6
- key_branch: bfloat16 [1024, 8192], P('tok', 'wid'), may hold values from -6 to 6
- value_branch: bfloat16 [1024, 8192], P('tok', 'wid'), may hold values from -6 to 6
- filters: float32 [512, 128], P('wid'), may hold values from -0.5 to 0.5
- out_weight: bfloat16 [8192, 8192], P(None, 'wid'), may hold values from -0.09375 to 0.09375
- cotangent: bfloat16 [1024, 8192], P('tok', 'wid'), may hold values from -6 to 6
Outputs:
- layer_out: bfloat16 [1024, 8192], P('tok', 'wid')
- grad_queries: bfloat16 [1024, 8192], P('tok', 'wid')
- grad_keys: bfloat16 [1024, 8192], P('tok', 'wid')
- grad_values: bfloat16 [1024, 8192], P('tok', 'wid')
- grad_filters: float32 [512, 128], P('wid')
All inputs are finite; a program needn't handle non-finite values.
Results may differ from a plain program's by a relative error of at most 0.02.
Values may be sent and summed in bfloat16 or wider, within the bound.
A program may use at most 192 MiB of HBM per device.

v0:
```python
import math
import jax
import jax.numpy as jnp
from jax import lax
from jax.sharding import PartitionSpec as P


def shifted(block, axis, distance):
    devices = range(lax.axis_size(axis))
    route = [(i - distance, i) for i in devices if i - distance in devices]
    return lax.ppermute(block, axis, route)


def causal_matrix(filters):
    groups, kernel = filters.shape
    span = 2 * kernel
    reverse = filters[:, ::-1]
    padded = jnp.concatenate(
        [
            jnp.zeros((groups, 1), jnp.float32),
            reverse,
            jnp.zeros((groups, span - kernel), jnp.float32),
        ],
        axis=1,
    )
    tiled = jnp.tile(padded, (1, kernel))[:, : kernel * span]
    return tiled.reshape(groups, kernel, span)


def split_pair(matrix):
    upper = matrix.astype(jnp.bfloat16)
    lower = (matrix - upper.astype(jnp.float32)).astype(jnp.bfloat16)
    return (upper, lower)


def split_einsum(form, pair, data):
    first = jnp.einsum(form, pair[0], data, preferred_element_type=jnp.float32)
    second = jnp.einsum(form, pair[1], data, preferred_element_type=jnp.float32)
    return first + second


def block_windows(extended, kernel, groups, group_size):
    blocks = extended.reshape(extended.shape[0] // kernel, kernel, groups, group_size)
    return jnp.concatenate([blocks[:-1], blocks[1:]], axis=1)


def gated_gradient(cotangent, out_weight):
    return (
        lax.psum_scatter(
            lax.dot_general(
                out_weight, cotangent, (((1,), (1,)), ((), ())), preferred_element_type=jnp.float32
            ).astype(jnp.bfloat16),
            "wid",
            scatter_dimension=0,
            tiled=True,
        )
        .astype(jnp.float32)
        .T
    )


def local(queries, key_branch, value_branch, filters, out_weight, cotangent):
    length, width = queries.shape
    groups, kernel = filters.shape
    group_size = width // groups
    nblocks = length // kernel
    kv = (key_branch.astype(jnp.float32) * value_branch.astype(jnp.float32)).astype(jnp.bfloat16)
    rim = shifted(kv, "tok", 1)
    extended = jnp.concatenate([rim, kv], axis=0)
    windows = block_windows(extended, kernel, groups, group_size)
    toeplitz = split_pair(causal_matrix(filters))
    conv = split_einsum("gts,bsgc->btgc", toeplitz, windows).reshape(length, width)
    gated = (queries.astype(jnp.float32) * conv).astype(jnp.bfloat16)
    layer_out = jnp.dot(
        lax.all_gather(gated, "wid", axis=1, tiled=True),
        out_weight,
        preferred_element_type=jnp.float32,
    ).astype(jnp.bfloat16)
    grad_gated = gated_gradient(cotangent, out_weight)
    grad_conv = (grad_gated * queries.astype(jnp.float32)).astype(jnp.bfloat16)
    grad_queries = (grad_gated * conv).astype(jnp.bfloat16)
    grad_blocks = grad_conv.reshape(nblocks, kernel, groups, group_size)
    spread = split_einsum("gts,btgc->bsgc", toeplitz, grad_blocks)
    lower_half = spread[:, :kernel]
    upper_half = spread[:, kernel:]
    returned = shifted(lower_half[0].reshape(kernel, width).astype(jnp.bfloat16), "tok", -1).astype(
        jnp.float32
    )
    tail = jnp.concatenate(
        [lower_half[1:], returned.reshape(1, kernel, groups, group_size)], axis=0
    )
    grad_kv = (upper_half + tail).reshape(length, width)
    grad_keys = (grad_kv * value_branch.astype(jnp.float32)).astype(jnp.bfloat16)
    grad_values = (grad_kv * key_branch.astype(jnp.float32)).astype(jnp.bfloat16)
    products = jnp.einsum(
        "btgc,bsgc->gts", grad_blocks, windows, preferred_element_type=jnp.float32
    )
    flat = jnp.pad(products.reshape(groups, kernel * 2 * kernel), ((0, 0), (0, kernel)))
    skewed = flat.reshape(groups, kernel, 2 * kernel + 1).sum(axis=1)
    local_terms = skewed[:, 1 : kernel + 1][:, ::-1]
    summed = lax.psum(local_terms, "tok")
    scale_factor = 1.0 / math.sqrt(length * lax.axis_size("tok") * group_size)
    grad_filters = summed * scale_factor
    return (layer_out, grad_queries, grad_keys, grad_values, grad_filters)


def solution(mesh):
    return jax.shard_map(
        local,
        mesh=mesh,
        in_specs=(
            P("tok", "wid"),
            P("tok", "wid"),
            P("tok", "wid"),
            P("wid", None),
            P(None, "wid"),
            P("tok", "wid"),
        ),
        out_specs=(
            P("tok", "wid"),
            P("tok", "wid"),
            P("tok", "wid"),
            P("tok", "wid"),
            P("wid", None),
        ),
        check_vma=False,
    )
```

profile of v0, /device:TPU:0, one launch (start us, length us, event | category | flops | bytes accessed | tf_op | source)
XLA Modules:
  0.0 323.4 jit_solution(6530451499667047419)
XLA Ops:
  8.2 16.6 %convolution_convert_fusion = bf16[8192,128]{1,0:T(8,128)(2,1)} fusion(bf16[8192,2048]{1,0:T(8,128)(2,1)} %param.10, bf16[128,2048]{1,0:T(8,128)(2,1)S(1)} %copy-done), kind=kOutput, calls=%fused_computation.1 | convolution fusion | flops 4296015872 | bytes 36175872 | tf_op jit(solution)/shard_map/dot_general | solution.py:50
  25.6 7.1 %tile.4 = f32[128,128,257]{0,2,1:T(8,128)} broadcast(f32[128,257]{0,1:T(8,128)S(1)} %copy.29), dimensions={0,2} | broadcast | bytes 16974336 | tf_op jit(solution)/shard_map/tile | solution.py:26
  32.7 17.8 %tile.10 = f32[128,32896]{0,1:T(8,128)} reshape(f32[128,128,257]{0,2,1:T(8,128)} %tile.4) | data formatting | bytes 33685504 | tf_op jit(solution)/shard_map/tile | solution.py:26
  50.5 11.4 %slice.27 = f32[128,32768]{0,1:T(8,128)} slice(f32[128,32896]{0,1:T(8,128)} %tile.10), slice={[0:128], [0:32768]} | slice | bytes 33554432 | tf_op jit(solution)/shard_map/slice | solution.py:26
  61.9 17.7 %copy.36 = f32[128,128,256]{2,1,0:T(8,128)} copy(f32[128,128,256]{0,2,1:T(8,128)} %bitcast.44) | data formatting | bytes 33554432 | tf_op jit(solution)/shard_map/reshape | solution.py:27
  79.6 1.2 fusion.1
  80.8 7.2 %fusion.11 = f32[128,16,256]{2,1,0:T(8,128)S(1)} fusion(bf16[128,128,16]{0,2,1:T(8,128)(2,1)S(1)} %bitcast.52, f32[128,128,256]{2,1,0:T(8,128)} %copy.36), kind=kOutput, calls=%fused_computation.27 | convolution fusion | flops 138412032 | bytes 19398656 | tf_op jit(solution)/shard_map/gts,btgc->bsgc/dot_general | solution.py:37
  88.0 3.5 %copy-done.2 = f32[128,128,256]{2,1,0:T(8,128)S(1)} copy-done((f32[128,128,256]{2,1,0:T(8,128)S(1)}, f32[128,128,256]{2,1,0:T(8,128)}, u32[]{:S(2)}) %copy-start.2) | copy-done | bytes 16777240
  91.5 1.2 add_bitcast_fusion
  92.8 1.3 collective-permute-start.1
  94.1 15.5 %collective-permute-done.1 = bf16[128,2048]{0,1:T(8,128)(2,1)S(1)} collective-permute-done((bf16[128,2048]{0,1:T(8,128)(2,1)S(1)}, bf16[128,2048]{0,1:T(8,128)(2,1)S(1)}, u32[]{:S(2)}, u32[]{:S(2)}) %collective-permute-start.1) | collective-permute-done | bytes 524320 | tf_op jit(solution)/shard_map/ppermute | solution.py:11
  110.1 2.4 fusion.2
  112.5 4.7 %collective-permute-start = (bf16[128,2048]{1,0:T(8,128)(2,1)S(1)}, bf16[128,2048]{1,0:T(8,128)(2,1)S(1)}, u32[]{:S(2)}, u32[]{:S(2)}) collective-permute-start(bf16[128,2048]{1,0:T(8,128)(2,1)S(1)} %get-tuple-element.22), channel_id=1, source_target_pairs={{0,4},{4,8},{8,12},{12,16},{16,20},{20,24},{24,28},{1,5},{5,9},{9,... | collective-permute-start | bytes 1572872 | tf_op jit(solution)/shard_map/ppermute | solution.py:11
  117.5 9.7 %collective-permute-done = bf16[128,2048]{1,0:T(8,128)(2,1)S(1)} collective-permute-done((bf16[128,2048]{1,0:T(8,128)(2,1)S(1)}, bf16[128,2048]{1,0:T(8,128)(2,1)S(1)}, u32[]{:S(2)}, u32[]{:S(2)}) %collective-permute-start) | collective-permute-done | bytes 524320 | tf_op jit(solution)/shard_map/ppermute | solution.py:11
  127.5 9.2 %fusion.7 = f32[128,16,128]{2,1,0:T(8,128)} fusion(bf16[1,128,128,16]{1,3,2,0:T(8,128)(2,1)S(1)} %bitcast.46, bf16[1,128,128,16]{1,3,2,0:T(8,128)(2,1)S(1)} %bitcast.49, f32[128,128,256]{2,1,0:T(8,128)} %copy.36), kind=kOutput, calls=%fused_computation.21 | convolution fusion | flops 140509184 | bytes 18874368 | tf_op jit(solution)/shard_map/gts,bsgc->btgc/dot_general | solution.py:37
  136.8 8.2 %fusion.6 = f32[128,128,256]{2,1,0:T(8,128)} fusion(bf16[128,128,16]{0,2,1:T(8,128)(2,1)S(1)} %bitcast.54, bf16[1,128,128,16]{1,3,2,0:T(8,128)(2,1)S(1)} %bitcast.47, bf16[1,128,128,16]{1,3,2,0:T(8,128)(2,1)S(1)} %bitcast.50), kind=kOutput, calls=%fused_computation.20 | convolution fusion | flops 136314880 | bytes 18350080 | tf_op jit(solution)/shard_map/btgc,bsgc->gts/dot_general | solution.py:95
  145.0 4.5 %convolution_add_fusion = f32[128,16,128]{2,1,0:T(8,128)} fusion(f32[128,16,128]{2,1,0:T(8,128)} %fusion.7, bf16[1,128,128,16]{1,3,2,0:T(8,128)(2,1)S(1)} %bitcast.48, bf16[1,128,128,16]{1,3,2,0:T(8,128)(2,1)S(1)} %bitcast.51, f32[128,128,256]{2,1,0:T(8,128)S(1)} %bitcast.43), kind=kOutput, calls=%fused_computation.4 | convolution fusion | flops 153354240 | bytes 19922944 | tf_op jit(solution)/shard_map/gts,bsgc->btgc/dot_general | solution.py:38
  149.5 17.9 %copy.37 = f32[128,128,256]{0,2,1:T(8,128)} copy(f32[128,128,256]{2,1,0:T(8,128)} %fusion.6) | data formatting | bytes 33554432 | tf_op jit(solution)/shard_map/reshape | solution.py:98
  167.4 13.3 %pad.4 = f32[128,32896]{0,1:T(8,128)} pad(f32[128,32768]{0,1:T(8,128)} %bitcast.45, f32[]{:T(128)} %constant.2.clone.1), padding=0_0x0_128 | pad | bytes 33619972 | tf_op jit(solution)/shard_map/jit(_pad)/pad | solution.py:98
  180.7 17.5 %reshape.67 = f32[128,128,257]{0,2,1:T(8,128)} reshape(f32[128,32896]{0,1:T(8,128)} %pad.4) | data formatting | bytes 33685504 | tf_op jit(solution)/shard_map/reshape | solution.py:99
  198.2 6.9 %reduce_sum.9 = f32[128,257]{0,1:T(8,128)S(1)} reduce(f32[128,128,257]{0,2,1:T(8,128)} %reshape.67, f32[]{:T(128)} %constant.2.clone.1), dimensions={1}, to_apply=%region_1.2 | reduce | flops 4177792 | bytes 16974340 | tf_op jit(solution)/shard_map/reduce_sum | solution.py:99
  208.0 67.5 %all-reduce.3.cloned.1.call-done = f32[128,128]{0,1:T(8,128)} async-done(((f32[128,128]{0,1:T(8,128)}), f32[128,128]{0,1:T(8,128)}) %all-reduce.3.cloned.1.call-update) | async-done | bytes 65552 | tf_op jit(solution)/shard_map/psum | solution.py:101
  277.1 23.2 %all-gather.2.cloned.1.call-done = bf16[128,8192]{0,1:T(8,128)(2,1)} async-done(((bf16[128,2048]{0,1:T(8,128)(2,1)}), bf16[128,8192]{0,1:T(8,128)(2,1)}) %all-gather.2.cloned.1.call-update) | async-done | bytes 2097168 | tf_op jit(solution)/shard_map/all_gather | solution.py:75
  300.4 16.5 %convolution_convert_fusion.1 = bf16[128,2048]{1,0:T(8,128)(2,1)} fusion(bf16[128,8192]{0,1:T(8,128)(2,1)} %all-gather.2.cloned.1.call-done, bf16[8192,2048]{1,0:T(8,128)(2,1)} %param.10), kind=kOutput, calls=%fused_computation.2 | convolution fusion | flops 4295229440 | bytes 36175872 | tf_op jit(solution)/shard_map/dot_general | solution.py:74
  (57 shorter events, 7.5 us)
Async XLA Ops:
  7.2 1.1 copy-start
  7.2 17.8 %copy-start.11 = (f32[128,128]{1,0:T(8,128)S(1)}, f32[128,128]{1,0:T(8,128)}, u32[]{:S(2)}) copy-start(f32[128,128]{1,0:T(8,128)} %param.9) | copy-start | bytes 196612
  7.2 18.1 %copy-start.10 = (bf16[128,2048]{1,0:T(8,128)(2,1)S(1)}, bf16[128,2048]{1,0:T(8,128)(2,1)}, u32[]{:S(2)}) copy-start(bf16[128,2048]{1,0:T(8,128)(2,1)} %param.6) | copy-start | bytes 1572868
  7.2 72.4 %reduce-scatter.2.cloned.1.call-start = ((), (), s32[]{:S(2)}) async-start(), calls=%async_computation.2 | async-start | bytes 2621440 | tf_op jit(solution)/shard_map/reduce_scatter | solution.py:49
  24.9 250.7 %all-reduce.3.cloned.1.call-start = ((), (), s32[]{:S(2)}) async-start(), calls=%async_computation.3 | async-start | bytes 131072 | tf_op jit(solution)/shard_map/psum | solution.py:101
  25.6 54.0 %copy-start.5 = (bf16[128,2048]{0,1:T(8,128)(2,1)}, bf16[128,2048]{0,1:T(8,128)(2,1)S(1)}, u32[]{:S(2)}) copy-start(bf16[128,2048]{0,1:T(8,128)(2,1)S(1)} %copy.26) | copy-start | bytes 1572868
  80.7 7.2 %copy-start.3 = (bf16[128,2048]{0,1:T(8,128)(2,1)}, bf16[128,2048]{0,1:T(8,128)(2,1)S(1)}, u32[]{:S(2)}) copy-start(bf16[128,2048]{0,1:T(8,128)(2,1)S(1)} %fusion.1) | copy-start | bytes 1572868
  80.8 10.7 %copy-start.2 = (f32[128,128,256]{2,1,0:T(8,128)S(1)}, f32[128,128,256]{2,1,0:T(8,128)}, u32[]{:S(2)}) copy-start(f32[128,128,256]{2,1,0:T(8,128)} %copy.36) | copy-start | bytes 50331652
  91.5 18.6 %copy-start.9 = (bf16[128,2048]{1,0:T(8,128)(2,1)S(1)}, bf16[128,2048]{1,0:T(8,128)(2,1)}, u32[]{:S(2)}) copy-start(bf16[128,2048]{1,0:T(8,128)(2,1)} %param.7) | copy-start | bytes 1572868
  92.8 16.8 %collective-permute-start.1 = (bf16[128,2048]{0,1:T(8,128)(2,1)S(1)}, bf16[128,2048]{0,1:T(8,128)(2,1)S(1)}, u32[]{:S(2)}, u32[]{:S(2)}) collective-permute-start(bf16[128,2048]{0,1:T(8,128)(2,1)S(1)} %bitcast.57), channel_id=1, source_target_pairs={{4,0},{8,4},{12,8},{16,12},{20,16},{24,20},{28,24},{5,1},{9,5},{13... | collective-permute-start | bytes 1572872 | tf_op jit(solution)/shard_map/ppermute | solution.py:11
  112.5 14.7 %collective-permute-start = (bf16[128,2048]{1,0:T(8,128)(2,1)S(1)}, bf16[128,2048]{1,0:T(8,128)(2,1)S(1)}, u32[]{:S(2)}, u32[]{:S(2)}) collective-permute-start(bf16[128,2048]{1,0:T(8,128)(2,1)S(1)} %get-tuple-element.22), channel_id=1, source_target_pairs={{0,4},{4,8},{8,12},{12,16},{16,20},{20,24},{24,28},{1,5},{5,9},{9,... | collective-permute-start | bytes 1572872 | tf_op jit(solution)/shard_map/ppermute | solution.py:11
  127.5 9.3 %copy-start.4 = (bf16[128,2048]{0,1:T(8,128)(2,1)S(1)}, bf16[128,2048]{0,1:T(8,128)(2,1)}, u32[]{:S(2)}) copy-start(bf16[128,2048]{0,1:T(8,128)(2,1)} %copy-done.3) | copy-start | bytes 1572868
  127.5 17.4 %slice-start = ((s8[16777216]{0:T(1024)(128)(4,1)}), s8[4194304]{0:T(1024)(128)(4,1)S(1)}, s32[]{:S(2)}) async-start(s8[16777216]{0:T(1024)(128)(4,1)} %bitcast.42), calls=%async_computation.4 | async-start | bytes 8388608
  127.5 17.4 %slice-start.1 = ((s8[16777216]{0:T(1024)(128)(4,1)}), s8[4194304]{0:T(1024)(128)(4,1)S(1)}, s32[]{:S(2)}) async-start(s8[16777216]{0:T(1024)(128)(4,1)} %bitcast.42), calls=%async_computation.5 | async-start | bytes 8388608
  127.5 17.4 %slice-start.2 = ((s8[16777216]{0:T(1024)(128)(4,1)}), s8[4194304]{0:T(1024)(128)(4,1)S(1)}, s32[]{:S(2)}) async-start(s8[16777216]{0:T(1024)(128)(4,1)} %bitcast.42), calls=%async_computation.6 | async-start | bytes 8388608
  136.8 8.2 %slice-start.3 = ((s8[16777216]{0:T(1024)(128)(4,1)}), s8[4194304]{0:T(1024)(128)(4,1)S(1)}, s32[]{:S(2)}) async-start(s8[16777216]{0:T(1024)(128)(4,1)} %bitcast.42), calls=%async_computation.7 | async-start | bytes 8388608
  198.1 7.8 %copy-start.6 = (bf16[128,2048]{0,1:T(8,128)(2,1)S(1)}, bf16[128,2048]{0,1:T(8,128)(2,1)}, u32[]{:S(2)}) copy-start(bf16[128,2048]{0,1:T(8,128)(2,1)} %copy-done.5) | copy-start | bytes 1572868
  198.1 7.8 %copy-start.7 = (f32[128,16,128]{2,1,0:T(8,128)S(1)}, f32[128,16,128]{2,1,0:T(8,128)}, u32[]{:S(2)}) copy-start(f32[128,16,128]{2,1,0:T(8,128)} %convolution_add_fusion) | copy-start | bytes 3145732
  198.2 7.8 %copy-start.8 = (bf16[2048,128]{1,0:T(8,128)(2,1)S(1)}, bf16[2048,128]{1,0:T(8,128)(2,1)}, u32[]{:S(2)}) copy-start(bf16[2048,128]{1,0:T(8,128)(2,1)} %reduce-scatter.2.cloned.1.call-done) | copy-start | bytes 1572868
  205.7 94.6 %all-gather.2.cloned.1.call-start = ((), (), s32[]{:S(2)}) async-start(), calls=%async_computation.1 | async-start | bytes 2621440 | tf_op jit(solution)/shard_map/all_gather | solution.py:75
  300.3 16.5 %copy-start.1 = (bf16[128,2048]{1,0:T(8,128)(2,1)S(1)}, bf16[128,2048]{1,0:T(8,128)(2,1)}, u32[]{:S(2)}) copy-start(bf16[128,2048]{1,0:T(8,128)(2,1)} %param.11) | copy-start | bytes 1572868
Sparse Core Ops, SparseCore 0:
  25.0 34.1 reduce-scatter.1
  205.8 69.7 all-reduce.2
  277.8 22.5 all-gather.1
where the time goes:
time: 325 us; the launch traced here: 323 us
  waiting for transfers between devices  116 us (36%)
  local copies, waits for them, and re-layouts  111 us (34%)
  matrix products  63.5 us (20%)
  between operations  14 us (4%)
  other arithmetic  12.5 us (4%)
  starting transfers between devices  6.37 us (2%)
    psum x1, waiting for transfers between devices, local(): summed = lax.psum(local_terms, 'tok')  67.5 us
    ppermute x2, waiting for transfers between devices, shifted(): return lax.ppermute(block, axis, route)  25.2 us
    another operation x2, local copies, waits for them, and re-layouts, causal_matrix(): tiled = jnp.tile(padded, (1, kernel))[:, :kernel * span]  24.9 us
    all_gather x1, waiting for transfers between devices, local(): lax.all_gather(gated, 'wid', axis=1, tiled=True)  23.2 us
    reshape x1, local copies, waits for them, and re-layouts, local(): products.reshape(groups, kernel * 2 * kernel)  17.9 us
    reshape x1, local copies, waits for them, and re-layouts, causal_matrix(): return tiled.reshape(groups, kernel, span)  17.7 us
    reshape x1, local copies, waits for them, and re-layouts, local(): skewed = flat.reshape(groups, kernel, 2 * kernel + 1).sum(axis=1)  17.5 us
    dot_general x1, matrix products, gated_gradient(): lax.dot_general(out_weight, cotangent, (((1,), (1,)), ((), ())), preferre...  16.6 us
  transfers between devices with their start and end apart: 5, of which 4 were waited for; matrix products, arithmetic and copies ran while one was open for 18% of the time, Pallas kernels for 0%

commit v1 on v0

--- a/solution.py
+++ b/solution.py
@@ -98,7 +98,7 @@
     flat = jnp.pad(products.reshape(groups, kernel * 2 * kernel), ((0, 0), (0, kernel)))
     skewed = flat.reshape(groups, kernel, 2 * kernel + 1).sum(axis=1)
     local_terms = skewed[:, 1 : kernel + 1][:, ::-1]
-    summed = lax.psum(local_terms, "tok")
+    summed = jnp.sum(lax.all_gather(local_terms, "tok"), axis=0)
     scale_factor = 1.0 / math.sqrt(length * lax.axis_size("tok") * group_size)
     grad_filters = summed * scale_factor
     return (layer_out, grad_queries, grad_keys, grad_values, grad_filters)

time: 325 us -> 276 us (0.85)
  waiting for transfers between devices: 116 us -> 25.2 us
  blocking collectives: 0 us -> 33 us
  matrix products: 63.5 us -> 71.1 us
    psum x1 -> x0, waiting for transfers between devices: 67.5 us -> none  [local(): summed = lax.psum(local_terms, 'tok')]
    all_gather x0 -> x1, blocking collectives: none -> 33 us  [local(): summed = jnp.sum(lax.all_gather(local_terms, 'tok'), axis=0)]
    all_gather x1, waiting for transfers between devices: 23.2 us -> 0.01 us  [local(): lax.all_gather(gated, 'wid', axis=1, tiled=True)]
    dot_general x2, matrix products: 5.75 us -> 14.1 us  [split_einsum(): second = jnp.einsum(form, pair[1], data, preferred_element_type=jnp.float32)]
    unnamed x35 -> x18, local copies, waits for them, and re-layouts: 6.57 us -> 6.51 us
  transfers between devices with their start and end apart: 5 -> 4, of which waited for: 4 -> 2; matrix products, arithmetic and copies ran while one was open for 18% -> 44% of each run, Pallas kernels for 0% -> 0%
where the time goes in v1:
time: 276 us; the launch traced here: 274 us
  local copies, waits for them, and re-layouts  112 us (41%)
  matrix products  71.1 us (26%)
  blocking collectives  33 us (12%)
  waiting for transfers between devices  25.2 us (9%)
  between operations  14.2 us (5%)
  other arithmetic  12.7 us (5%)
  starting transfers between devices  6.11 us (2%)
    all_gather x1, blocking collectives, local(): summed = jnp.sum(lax.all_gather(local_terms, 'tok'), axis=0)  33 us
    ppermute x2, waiting for transfers between devices, shifted(): return lax.ppermute(block, axis, route)  25.2 us
    another operation x2, local copies, waits for them, and re-layouts, causal_matrix(): tiled = jnp.tile(padded, (1, kernel))[:, :kernel * span]  24.9 us
    reshape x1, local copies, waits for them, and re-layouts, local(): products.reshape(groups, kernel * 2 * kernel)  17.9 us
    reshape x1, local copies, waits for them, and re-layouts, causal_matrix(): return tiled.reshape(groups, kernel, span)  17.7 us
    reshape x1, local copies, waits for them, and re-layouts, local(): skewed = flat.reshape(groups, kernel, 2 * kernel + 1).sum(axis=1)  17.5 us
    dot_general x1, matrix products, gated_gradient(): lax.dot_general(out_weight, cotangent, (((1,), (1,)), ((), ())), preferre...  16.6 us
    dot_general x1, matrix products, local(): jnp.dot(lax.all_gather(gated, 'wid', axis=1, tiled=True), out_weight, pre...  16.5 us
  transfers between devices with their start and end apart: 4, of which 2 were waited for; matrix products, arithmetic and copies ran while one was open for 44% of the time, Pallas kernels for 0%

profile of v1, /device:TPU:0, one launch (start us, length us, event | category | flops | bytes accessed | tf_op | source)
XLA Modules:
  0.0 273.9 jit_solution(13379779544495700143)
XLA Ops:
  8.2 16.6 %convolution_convert_fusion = bf16[8192,128]{1,0:T(8,128)(2,1)} fusion(bf16[8192,2048]{1,0:T(8,128)(2,1)} %param.10, bf16[128,2048]{1,0:T(8,128)(2,1)S(1)} %copy-done), kind=kOutput, calls=%fused_computation.1 | convolution fusion | flops 4296015872 | bytes 36175872 | tf_op jit(solution)/shard_map/dot_general | solution.py:50
  25.6 7.1 %tile.4 = f32[128,128,257]{0,2,1:T(8,128)} broadcast(f32[128,257]{0,1:T(8,128)S(1)} %copy.38), dimensions={0,2} | broadcast | bytes 16974336 | tf_op jit(solution)/shard_map/tile | solution.py:26
  32.7 17.8 %tile.10 = f32[128,32896]{0,1:T(8,128)} reshape(f32[128,128,257]{0,2,1:T(8,128)} %tile.4) | data formatting | bytes 33685504 | tf_op jit(solution)/shard_map/tile | solution.py:26
  50.5 11.4 %slice.27 = f32[128,32768]{0,1:T(8,128)} slice(f32[128,32896]{0,1:T(8,128)} %tile.10), slice={[0:128], [0:32768]} | slice | bytes 33554432 | tf_op jit(solution)/shard_map/slice | solution.py:26
  61.9 17.7 %copy.45 = f32[128,128,256]{2,1,0:T(8,128)} copy(f32[128,128,256]{0,2,1:T(8,128)} %bitcast.47) | data formatting | bytes 33554432 | tf_op jit(solution)/shard_map/reshape | solution.py:27
  79.6 1.2 fusion.1
  80.7 7.1 %fusion.11 = f32[128,16,256]{2,1,0:T(8,128)S(1)} fusion(bf16[128,128,16]{0,2,1:T(8,128)(2,1)S(1)} %bitcast.55, f32[128,128,256]{2,1,0:T(8,128)} %copy.45), kind=kOutput, calls=%fused_computation.28 | convolution fusion | flops 138412032 | bytes 19398656 | tf_op jit(solution)/shard_map/gts,btgc->bsgc/dot_general | solution.py:37
  87.9 3.4 %copy-done.2 = f32[128,128,256]{2,1,0:T(8,128)S(1)} copy-done((f32[128,128,256]{2,1,0:T(8,128)S(1)}, f32[128,128,256]{2,1,0:T(8,128)}, u32[]{:S(2)}) %copy-start.2) | copy-done | bytes 16777240
  91.3 1.2 add_bitcast_fusion
  92.6 1.3 collective-permute-start.1
  93.9 15.5 %collective-permute-done.1 = bf16[128,2048]{0,1:T(8,128)(2,1)S(1)} collective-permute-done((bf16[128,2048]{0,1:T(8,128)(2,1)S(1)}, bf16[128,2048]{0,1:T(8,128)(2,1)S(1)}, u32[]{:S(2)}, u32[]{:S(2)}) %collective-permute-start.1) | collective-permute-done | bytes 524320 | tf_op jit(solution)/shard_map/ppermute | solution.py:11
  110.5 1.6 copy.40
  112.1 2.4 fusion.2
  114.5 4.7 %collective-permute-start = (bf16[128,2048]{1,0:T(8,128)(2,1)S(1)}, bf16[128,2048]{1,0:T(8,128)(2,1)S(1)}, u32[]{:S(2)}, u32[]{:S(2)}) collective-permute-start(bf16[128,2048]{1,0:T(8,128)(2,1)S(1)} %get-tuple-element.27), channel_id=1, source_target_pairs={{0,4},{4,8},{8,12},{12,16},{16,20},{20,24},{24,28},{1,5},{5,9},{9,... | collective-permute-start | bytes 1572872 | tf_op jit(solution)/shard_map/ppermute | solution.py:11
  119.5 9.7 %collective-permute-done = bf16[128,2048]{1,0:T(8,128)(2,1)S(1)} collective-permute-done((bf16[128,2048]{1,0:T(8,128)(2,1)S(1)}, bf16[128,2048]{1,0:T(8,128)(2,1)S(1)}, u32[]{:S(2)}, u32[]{:S(2)}) %collective-permute-start) | collective-permute-done | bytes 524320 | tf_op jit(solution)/shard_map/ppermute | solution.py:11
  129.4 8.1 %fusion.7 = f32[128,16,128]{2,1,0:T(8,128)S(1)} fusion(bf16[1,128,128,16]{1,3,2,0:T(8,128)(2,1)S(1)} %bitcast.49, bf16[1,128,128,16]{1,3,2,0:T(8,128)(2,1)S(1)} %bitcast.52, f32[128,128,256]{2,1,0:T(8,128)} %copy.45), kind=kOutput, calls=%fused_computation.22 | convolution fusion | flops 140509184 | bytes 18874368 | tf_op jit(solution)/shard_map/gts,bsgc->btgc/dot_general | solution.py:37
  137.5 12.9 %convolution_add_fusion = f32[128,16,128]{2,1,0:T(8,128)S(1)} fusion(f32[128,16,128]{2,1,0:T(8,128)S(1)} %fusion.7, bf16[1,128,128,16]{1,3,2,0:T(8,128)(2,1)S(1)} %bitcast.50, bf16[1,128,128,16]{1,3,2,0:T(8,128)(2,1)S(1)} %bitcast.53, f32[128,128,256]{2,1,0:T(8,128)} %copy.45), kind=kOutput, calls=%fused_computation.4 | convolution fusion | flops 153354240 | bytes 19922944 | tf_op jit(solution)/shard_map/gts,bsgc->btgc/dot_general | solution.py:38
  152.5 8.6 %fusion.6 = f32[128,128,256]{2,1,0:T(8,128)} fusion(bf16[128,128,16]{0,2,1:T(8,128)(2,1)S(1)} %bitcast.57, bf16[1,128,128,16]{1,3,2,0:T(8,128)(2,1)S(1)} %bitcast.51, bf16[1,128,128,16]{1,3,2,0:T(8,128)(2,1)S(1)} %bitcast.54), kind=kOutput, calls=%fused_computation.21 | convolution fusion | flops 136314880 | bytes 18350080 | tf_op jit(solution)/shard_map/btgc,bsgc->gts/dot_general | solution.py:95
  161.1 17.9 %copy.46 = f32[128,128,256]{0,2,1:T(8,128)} copy(f32[128,128,256]{2,1,0:T(8,128)} %fusion.6) | data formatting | bytes 33554432 | tf_op jit(solution)/shard_map/reshape | solution.py:98
  179.0 13.3 %pad.4 = f32[128,32896]{0,1:T(8,128)} pad(f32[128,32768]{0,1:T(8,128)} %bitcast.48, f32[]{:T(128)} %constant.2.clone.1), padding=0_0x0_128 | pad | bytes 33619972 | tf_op jit(solution)/shard_map/jit(_pad)/pad | solution.py:98
  192.3 17.5 %reshape.67 = f32[128,128,257]{0,2,1:T(8,128)} reshape(f32[128,32896]{0,1:T(8,128)} %pad.4) | data formatting | bytes 33685504 | tf_op jit(solution)/shard_map/reshape | solution.py:99
  209.8 6.7 %reduce_sum.18 = f32[128,257]{0,1:T(8,128)S(1)} reduce(f32[128,128,257]{0,2,1:T(8,128)} %reshape.67, f32[]{:T(128)} %constant.2.clone.1), dimensions={1}, to_apply=%region_1.2 | reduce | flops 4177792 | bytes 16974340 | tf_op jit(solution)/shard_map/reduce_sum | solution.py:99
  216.6 33.0 %all-gather = f32[1024,128]{0,1:T(8,128)S(1)} all-gather(f32[128,128]{0,1:T(8,128)S(1)} %rev.7), channel_id=2, replica_groups=mesh['tok'=8,'wid'=4] {'tok'}, dimensions={0}, use_global_device_ids=true | all-gather | bytes 589824 | tf_op jit(solution)/shard_map/all_gather | solution.py:101
  250.5 16.5 %convolution_convert_fusion.1 = bf16[128,2048]{1,0:T(8,128)(2,1)} fusion(bf16[128,8192]{0,1:T(8,128)(2,1)} %all-gather.3.cloned.1.call-done, bf16[8192,2048]{1,0:T(8,128)(2,1)} %param.10), kind=kOutput, calls=%fused_computation.2 | convolution fusion | flops 4295229440 | bytes 36175872 | tf_op jit(solution)/shard_map/dot_general | solution.py:74
  (38 shorter events, 6.6 us)
Async XLA Ops:
  7.2 1.1 copy-start
  7.2 17.8 %copy-start.6 = (f32[128,128]{1,0:T(8,128)S(1)}, f32[128,128]{1,0:T(8,128)}, u32[]{:S(2)}) copy-start(f32[128,128]{1,0:T(8,128)} %param.9) | copy-start | bytes 196612
  7.2 18.1 %copy-start.5 = (bf16[128,2048]{1,0:T(8,128)(2,1)S(1)}, bf16[128,2048]{1,0:T(8,128)(2,1)}, u32[]{:S(2)}) copy-start(bf16[128,2048]{1,0:T(8,128)(2,1)} %param.6) | copy-start | bytes 1572868
  7.2 72.3 %reduce-scatter.2.cloned.1.call-start = ((), (), s32[]{:S(2)}) async-start(), calls=%async_computation.2 | async-start | bytes 2621440 | tf_op jit(solution)/shard_map/reduce_scatter | solution.py:49
  24.9 225.7 %all-gather.3.cloned.1.call-start = ((), (), s32[]{:S(2)}) async-start(), calls=%async_computation.1 | async-start | bytes 2621440 | tf_op jit(solution)/shard_map/all_gather | solution.py:75
  80.7 10.5 %copy-start.2 = (f32[128,128,256]{2,1,0:T(8,128)S(1)}, f32[128,128,256]{2,1,0:T(8,128)}, u32[]{:S(2)}) copy-start(f32[128,128,256]{2,1,0:T(8,128)} %copy.45) | copy-start | bytes 50331652
  91.3 20.8 %copy-start.4 = (bf16[128,2048]{1,0:T(8,128)(2,1)S(1)}, bf16[128,2048]{1,0:T(8,128)(2,1)}, u32[]{:S(2)}) copy-start(bf16[128,2048]{1,0:T(8,128)(2,1)} %param.7) | copy-start | bytes 1572868
  92.6 16.8 %collective-permute-start.1 = (bf16[128,2048]{0,1:T(8,128)(2,1)S(1)}, bf16[128,2048]{0,1:T(8,128)(2,1)S(1)}, u32[]{:S(2)}, u32[]{:S(2)}) collective-permute-start(bf16[128,2048]{0,1:T(8,128)(2,1)S(1)} %bitcast.61), channel_id=1, source_target_pairs={{4,0},{8,4},{12,8},{16,12},{20,16},{24,20},{28,24},{5,1},{9,5},{13... | collective-permute-start | bytes 1572872 | tf_op jit(solution)/shard_map/ppermute | solution.py:11
  114.5 14.7 %collective-permute-start = (bf16[128,2048]{1,0:T(8,128)(2,1)S(1)}, bf16[128,2048]{1,0:T(8,128)(2,1)S(1)}, u32[]{:S(2)}, u32[]{:S(2)}) collective-permute-start(bf16[128,2048]{1,0:T(8,128)(2,1)S(1)} %get-tuple-element.27), channel_id=1, source_target_pairs={{0,4},{4,8},{8,12},{12,16},{16,20},{20,24},{24,28},{1,5},{5,9},{9,... | collective-permute-start | bytes 1572872 | tf_op jit(solution)/shard_map/ppermute | solution.py:11
  137.5 12.9 %copy-start.3 = (bf16[2048,128]{1,0:T(8,128)(2,1)S(1)}, bf16[2048,128]{1,0:T(8,128)(2,1)}, u32[]{:S(2)}) copy-start(bf16[2048,128]{1,0:T(8,128)(2,1)} %reduce-scatter.2.cloned.1.call-done) | copy-start | bytes 1572868
  250.5 16.6 %copy-start.1 = (bf16[128,2048]{1,0:T(8,128)(2,1)S(1)}, bf16[128,2048]{1,0:T(8,128)(2,1)}, u32[]{:S(2)}) copy-start(bf16[128,2048]{1,0:T(8,128)(2,1)} %param.11) | copy-start | bytes 1572868
Sparse Core Ops, SparseCore 0:
  25.0 34.1 reduce-scatter.1
  151.6 23.7 all-gather.2
